TPU v7x, 1024 devices: a whole 4x4x32 slice. The times are simulated.
1024 devices in a mesh: row: 8 (over y, core), col: 128 (over z, x).
Axes of the slice: x: 4, y: 4, z: 32, core: 2. Of those that a mesh axis runs over, the one named last changes fastest.
Arguments:
- conc: float32 [118784, 512], P(('row', 'col')), may hold values from -1 to 1
- levels: int32 [118784], P(('row', 'col')), may hold values from 0 to 2
- neighbours: int32 [6, 118784], P(None, ('row', 'col')), may hold values from -1 to 98303, as said below
- hanging: int32 [6, 118784], P(None, ('row', 'col')), may hold values 0 or 1
- block_counts: int32 [1024], replicated, may hold values from 76 to 116, as said below
Outputs:
- conc_next: float32 [118784, 512], P(('row', 'col'))
- potential: float32 [118784, 512], P(('row', 'col'))
Inputs may be any that keep to these rules, and one draw needn't show every extreme that they name: `neighbours`: slots at or past a device's count hold -1. A live block's faces name live blocks, matched: if block a's face f names b, then b's face f xor 1 names a. A named block lies on the same device, on another device of the same row, or on the device of the same col in the row before or after (rows taken periodically). Between two devices of one row, in each direction, either no face or exactly 2 faces cross. Between a device and the device of the same col in the next row, 1 to 16 matched face pairs come in each direction's pair count, so 2 to 32 faces cross each way, 32 in some pairs of every draw. `block_counts`: the counts sum to 98304; the largest is 116.
All inputs are finite; a program needn't handle non-finite values. No bound on the sum of `hanging` on one device may be relied on, other than what follows from the above.
Results may differ from a plain program's by a relative error of at most 0.00005.
Values sent between devices are 32-bit elements; how exact they have to be, the bound alone decides.
A program may use at most 32 MiB of HBM per device.

v0:
```python
import jax
import jax.numpy as jnp
from jax import lax
from jax.sharding import PartitionSpec as P

KMAX = 16
MOST = 2


gradient_energy = 0.0625
time_step = 0.0004


def with_halo(block, sides, width):
    for axis, dim in sides:
        count = lax.axis_size(axis)
        forward = [(i, i + 1) for i in range(count - 1)]
        forward.append((count - 1, 0))
        backward = [(target, source) for source, target in forward]
        low = lax.ppermute(
            lax.slice_in_dim(block, block.shape[dim] - width, None, axis=dim), axis, forward
        )
        high = lax.ppermute(lax.slice_in_dim(block, 0, width, axis=dim), axis, backward)
        block = jnp.concatenate([low, block, high], axis=dim)
    return block


def selection_table():
    entry_id = jnp.arange(64, dtype=jnp.int32)
    first_part = entry_id // 8
    second_part = entry_id % 8
    face_cells = jnp.stack(
        [
            entry_id,
            448 + entry_id,
            first_part * 64 + second_part,
            first_part * 64 + 56 + second_part,
            first_part * 64 + second_part * 8,
            first_part * 64 + second_part * 8 + 7,
        ]
    ).reshape(384)
    cell_id = jnp.arange(512, dtype=jnp.int32)
    return jnp.where(cell_id[:, None] == face_cells[None, :], 1.0, 0.0).astype(jnp.float32)


def averaging_table():
    entry_id = jnp.arange(64, dtype=jnp.int32)
    group_id = entry_id // 16 * 4 + entry_id % 8 // 2
    return jnp.where(group_id[:, None] == group_id[None, :], 0.25, 0.0).astype(jnp.float32)


def neighbour_sum(field):
    cell_id = jnp.arange(512, dtype=jnp.int32)[None, :]
    coordinates = (cell_id // 64, cell_id // 8 % 8, cell_id % 8)
    strides = (64, 8, 1)
    summed = jnp.zeros_like(field)
    for direction in range(3):
        stride = strides[direction]
        position = coordinates[direction]
        summed = summed + jnp.where(position > 0, jnp.roll(field, stride, axis=1), 0.0)
        summed = summed + jnp.where(position < 7, jnp.roll(field, -stride, axis=1), 0.0)
    return summed


def ranked(partner, order_key, selected_entries, key_span, sentinel):
    composite = jnp.where(selected_entries, partner * key_span + order_key, sentinel).reshape(-1)
    ordering_index = jnp.argsort(composite)
    sorted_keys = composite[ordering_index]
    position = (
        jnp.zeros_like(composite)
        .at[ordering_index]
        .set(jnp.arange(composite.shape[0], dtype=jnp.int32))
    )
    first_seen = jnp.searchsorted(sorted_keys, (partner * key_span).reshape(-1))
    return (position - first_seen).reshape(partner.shape)


def per_device(conc, levels, neighbours, hanging, block_counts):
    blocks = conc.shape[0]
    col_count = lax.axis_size("col")
    row_count = lax.axis_size("row")
    my_row = lax.axis_index("row")
    my_col = lax.axis_index("col")
    my_device = my_row * col_count + my_col
    offsets = jnp.cumsum(block_counts) - block_counts
    is_live = jnp.arange(blocks, dtype=jnp.int32) < block_counts[my_device]
    face_indices = jnp.arange(6, dtype=jnp.int32)[None, :]
    slot_ids = jnp.arange(blocks, dtype=jnp.int32)[:, None]
    named_blocks = neighbours.T
    usable = is_live[:, None] & (named_blocks >= 0)
    target = jnp.where(usable, named_blocks, offsets[my_device])
    owner_dev = jnp.searchsorted(offsets, target, side="right") - 1
    holder_slot_index = target - offsets[owner_dev]
    owner_row = owner_dev // col_count
    owner_col = owner_dev % col_count
    elsewhere = usable & (owner_dev != my_device)
    same_row = elsewhere & (owner_row == my_row)
    from_below = elsewhere & ~same_row & (owner_row == (my_row + row_count - 1) % row_count)
    from_above = elsewhere & ~same_row & ~from_below
    partner = jnp.where(same_row, owner_col, jnp.where(from_below, col_count, col_count + 1))
    key_span = 6 * blocks
    sentinel = (col_count + 2) * key_span
    opposite = jnp.bitwise_xor(face_indices, 1)
    take_rank = ranked(partner, holder_slot_index * 6 + opposite, elsewhere, key_span, sentinel)
    give_rank = ranked(partner, slot_ids * 6 + face_indices, elsewhere, key_span, sentinel)
    slab_slots = 2 * KMAX
    own_rows = (slot_ids * 6 + face_indices).reshape(-1)
    far_where = jnp.where(same_row, owner_col * MOST + give_rank, col_count * MOST).reshape(-1)
    far_source = jnp.zeros((col_count * MOST,), jnp.int32).at[far_where].set(own_rows, mode="drop")
    down_where = jnp.where(from_below, give_rank, slab_slots).reshape(-1)
    down_source = jnp.zeros((slab_slots,), jnp.int32).at[down_where].set(own_rows, mode="drop")
    up_where = jnp.where(from_above, give_rank, slab_slots).reshape(-1)
    up_source = jnp.zeros((slab_slots,), jnp.int32).at[up_where].set(own_rows, mode="drop")
    base_row = 6 * blocks
    ghost_rows = jnp.where(
        same_row,
        base_row + owner_col * MOST + take_rank,
        jnp.where(
            from_below,
            base_row + col_count * MOST + take_rank,
            jnp.where(
                from_above,
                base_row + col_count * MOST + slab_slots + take_rank,
                holder_slot_index * 6 + opposite,
            ),
        ),
    ).reshape(-1)
    coarse_mask = (hanging.T > 0).reshape(-1, 1)
    inverse_square = jnp.left_shift(jnp.int32(1), 2 * levels).astype(jnp.float32)
    averaging = averaging_table()
    selection = selection_table()
    spreading = selection.T

    def laplacian(field):
        records = jnp.dot(field, selection, precision=lax.Precision.HIGHEST).reshape(blocks * 6, 64)
        departing_faces = records[far_source].reshape(col_count, MOST * 64)
        incoming = lax.all_to_all(departing_faces, "col", split_axis=0, concat_axis=0, tiled=True)
        slab_out = jnp.stack([records[down_source].reshape(-1), records[up_source].reshape(-1)])
        slab_in = with_halo(slab_out, (("row", 0),), 1)
        sources = jnp.concatenate(
            [
                records,
                incoming.reshape(col_count * MOST, 64),
                slab_in[0].reshape(slab_slots, 64),
                slab_in[3].reshape(slab_slots, 64),
            ],
            axis=0,
        )
        ghosts = sources[ghost_rows]
        coarse = jnp.dot(ghosts, averaging, precision=lax.Precision.HIGHEST)
        ghosts = jnp.where(coarse_mask, coarse, ghosts).reshape(blocks, 384)
        beyond = jnp.dot(ghosts, spreading, precision=lax.Precision.HIGHEST)
        return (neighbour_sum(field) + beyond - 6.0 * field) * inverse_square[:, None]

    first_mu = conc * conc * conc - conc - gradient_energy * laplacian(conc)
    section_conc = conc + time_step * laplacian(first_mu)
    second_mu = (
        section_conc * section_conc * section_conc
        - section_conc
        - gradient_energy * laplacian(section_conc)
    )
    finished = 0.5 * (conc + section_conc + time_step * laplacian(second_mu))
    keep = is_live[:, None]
    return (jnp.where(keep, finished, 0.0), jnp.where(keep, second_mu, 0.0))


def solution(mesh):
    return jax.shard_map(
        per_device,
        mesh=mesh,
        in_specs=(
            P(("row", "col"), None),
            P(("row", "col")),
            P(None, ("row", "col")),
            P(None, ("row", "col")),
            P(),
        ),
        out_specs=(P(("row", "col"), None), P(("row", "col"), None)),
        check_vma=False,
    )
```

profile of v0, /device:TPU:24, one launch (start us, length us, event | category | flops | bytes accessed | tf_op | source)
XLA Modules:
  0.0 334.5 jit_solution(14700722400374067885)
XLA Ops:
  5.0 37.6 %while.64 = (s32[]{:T(128)}, u32[116,6]{1,0:T(8,128)S(1)}, u32[116,6]{1,0:T(8,128)S(1)}, s32[1024]{0:T(1024)S(1)}, s32[116,6]{1,0:T(8,128)S(1)}, /*index=5*/s32[]{:T(128)}, s32[]{:T(128)}, s32[]{}) while((s32[]{:T(128)}, u32[116,6]{1,0:T(8,128)S(1)}, u32[116,6]{1,0:T(8,128)S(1)}, s32[1024]{0:T(1024)S(1)}, s32[116,6]{1,0:T(8,128)S(1)}, ...), condition=%wide.region_3.4_spmd.clone, body=%wide.region_2.3_spmd.clone.sunk | while | flops 13556 | bytes 64061 | solution.py:92
  5.2 3.0 gather_fusion
  8.6 3.0 gather_fusion
  12.0 3.0 gather_fusion
  15.4 3.0 gather_fusion
  18.8 3.0 gather_fusion
  22.3 3.0 gather_fusion
  25.7 3.0 gather_fusion
  29.1 3.0 gather_fusion
  32.5 3.0 gather_fusion
  35.9 3.0 gather_fusion
  39.4 3.0 gather_fusion
  42.8 3.0 gather_fusion.7
  47.0 4.4 %sort.32 = (s32[696]{0:T(1024)}, s32[696]{0:T(1024)S(1)}) sort(s32[696]{0:T(1024)S(1)} %reshape.510, s32[696]{0:T(1024)S(1)} %iota.170), dimensions={0}, to_apply=%region_11.12 | sort | flops 6960 | bytes 11136 | tf_op jit(solution)/shard_map/jit(argsort)/sort | solution.py:67
  51.4 4.1 %scatter_custom_fusion.4 = s32[696]{0:T(1024)S(1)} fusion(s32[696]{0:T(1024)S(1)} %compare_select_fusion.4, s32[696]{0:T(1024)S(1)} %iota.171, s32[]{:T(128)} %constant.291.clone.1), kind=kCustom, calls=%fused_computation.256 | custom fusion | bytes 2788 | tf_op jit(solution)/shard_map/scatter | solution.py:72
  55.5 3.0 gather_fusion.8
  58.5 30.8 %while.66 = (s32[]{:T(128)}, u32[696]{0:T(1024)S(1)}, u32[696]{0:T(1024)S(1)}, s32[696]{0:T(1024)S(1)}, s32[696]{0:T(1024)S(1)}, /*index=5*/s32[]{:T(128)}, s32[]{:T(128)}, s32[]{}) while((s32[]{:T(128)}, u32[696]{0:T(1024)S(1)}, u32[696]{0:T(1024)S(1)}, s32[696]{0:T(1024)S(1)}, s32[696]{0:T(1024)S(1)}, /*index=5*/s32[]{:T(128)}, ...), condition=%wide.region_14.15_spmd.clone, body=%wide.region_13.14_spmd.clone.sunk | while | flops 13556 | bytes 52925 | solution.py:74
  58.6 3.0 gather_fusion.2
  61.6 3.0 gather_fusion.2
  64.7 3.0 gather_fusion.2
  67.8 3.0 gather_fusion.2
  70.9 3.0 gather_fusion.2
  74.0 3.0 gather_fusion.2
  77.1 3.0 gather_fusion.2
  80.1 3.0 gather_fusion.2
  83.2 3.0 gather_fusion.2
  86.3 3.0 gather_fusion.2
  89.9 4.4 %sort.31 = (s32[696]{0:T(1024)}, s32[696]{0:T(1024)S(1)}) sort(s32[696]{0:T(1024)S(1)} %reshape.503, s32[696]{0:T(1024)S(1)} %iota.167), dimensions={0}, to_apply=%region_4.5 | sort | flops 6960 | bytes 11136 | tf_op jit(solution)/shard_map/jit(argsort)/sort | solution.py:67
  94.3 4.1 %scatter_custom_fusion = s32[696]{0:T(1024)S(1)} fusion(s32[696]{0:T(1024)S(1)} %compare_select_fusion.5, s32[696]{0:T(1024)S(1)} %iota.168, s32[]{:T(128)} %constant.291.clone.1), kind=kCustom, calls=%fused_computation.258 | custom fusion | bytes 2788 | tf_op jit(solution)/shard_map/scatter | solution.py:72
  98.4 3.0 gather_fusion.3
  101.4 30.8 %while.65 = (s32[]{:T(128)}, u32[696]{0:T(1024)S(1)}, u32[696]{0:T(1024)S(1)}, s32[696]{0:T(1024)S(1)}, s32[696]{0:T(1024)S(1)}, /*index=5*/s32[]{:T(128)}, s32[]{:T(128)}, s32[]{}) while((s32[]{:T(128)}, u32[696]{0:T(1024)S(1)}, u32[696]{0:T(1024)S(1)}, s32[696]{0:T(1024)S(1)}, s32[696]{0:T(1024)S(1)}, /*index=5*/s32[]{:T(128)}, ...), condition=%wide.region_7.8_spmd.clone, body=%wide.region_6.7_spmd.clone.sunk | while | flops 13556 | bytes 52925 | solution.py:74
  101.4 3.0 gather_fusion.1
  104.5 3.0 gather_fusion.1
  107.6 3.0 gather_fusion.1
  110.7 3.0 gather_fusion.1
  113.8 3.0 gather_fusion.1
  116.8 3.0 gather_fusion.1
  133.4 4.1 %scatter_custom_fusion.2 = s32[32]{0:T(128)S(1)} fusion(s32[696]{0:T(1024)S(1)} %fusion.161, s32[696]{0:T(1024)S(1)} %reshape.727, s32[]{:T(128)} %constant.291.clone.1), kind=kCustom, calls=%fused_computation.293 | custom fusion | bytes 132 | tf_op jit(solution)/shard_map/scatter | solution.py:113
  139.2 4.3 %scatter_custom_fusion.3 = s32[32]{0:T(128)S(1)} fusion(s32[696]{0:T(1024)S(1)} %fusion.162, s32[696]{0:T(1024)S(1)} %reshape.727, s32[]{:T(128)} %constant.291.clone.1), kind=kCustom, calls=%fused_computation.291 | custom fusion | bytes 132 | tf_op jit(solution)/shard_map/scatter | solution.py:111
  146.1 4.1 %scatter_custom_fusion.1 = s32[256]{0:T(256)S(1)} fusion(s32[696]{0:T(1024)S(1)} %fusion.160, s32[696]{0:T(1024)S(1)} %reshape.727, s32[]{:T(128)} %constant.291.clone.1), kind=kCustom, calls=%fused_computation.285 | custom fusion | bytes 1028 | tf_op jit(solution)/shard_map/scatter | solution.py:109
  151.7 33.0 %all-to-all-start = ((f32[128,1,128]{2,1,0:T(1,128)}), f32[128,1,128]{2,1,0:T(1,128)S(1)}, u32[]{:S(2)}, u32[]{:S(2)}) async-start(f32[128,1,128]{2,1,0:T(1,128)} %bitcast.7), calls=%async_computation | async-start | bytes 131072 | tf_op jit(solution)/shard_map/all_to_all | solution.py:137
  188.5 20.9 %all-to-all-done = f32[128,1,128]{2,1,0:T(1,128)S(1)} async-done(((f32[128,1,128]{2,1,0:T(1,128)}), f32[128,1,128]{2,1,0:T(1,128)S(1)}, u32[]{:S(2)}, u32[]{:S(2)}) %all-to-all-start) | async-done | bytes 65568 | tf_op jit(solution)/shard_map/all_to_all | solution.py:137
  216.9 6.4 %all-to-all-start.1 = ((f32[128,1,128]{2,1,0:T(1,128)}), f32[128,1,128]{2,1,0:T(1,128)S(1)}, u32[]{:S(2)}, u32[]{:S(2)}) async-start(f32[128,1,128]{2,1,0:T(1,128)} %bitcast.8), calls=%async_computation.1 | async-start | bytes 131072 | tf_op jit(solution)/shard_map/all_to_all | solution.py:137
  229.2 18.3 %all-to-all-done.1 = f32[128,1,128]{2,1,0:T(1,128)S(1)} async-done(((f32[128,1,128]{2,1,0:T(1,128)}), f32[128,1,128]{2,1,0:T(1,128)S(1)}, u32[]{:S(2)}, u32[]{:S(2)}) %all-to-all-start.1) | async-done | bytes 65568 | tf_op jit(solution)/shard_map/all_to_all | solution.py:137
  254.9 7.2 %all-to-all-start.2 = ((f32[128,1,128]{2,1,0:T(1,128)}), f32[128,1,128]{2,1,0:T(1,128)S(1)}, u32[]{:S(2)}, u32[]{:S(2)}) async-start(f32[128,1,128]{2,1,0:T(1,128)} %bitcast.9), calls=%async_computation.2 | async-start | bytes 131072 | tf_op jit(solution)/shard_map/all_to_all | solution.py:137
  268.0 19.0 %all-to-all-done.2 = f32[128,1,128]{2,1,0:T(1,128)S(1)} async-done(((f32[128,1,128]{2,1,0:T(1,128)}), f32[128,1,128]{2,1,0:T(1,128)S(1)}, u32[]{:S(2)}, u32[]{:S(2)}) %all-to-all-start.2) | async-done | bytes 65568 | tf_op jit(solution)/shard_map/all_to_all | solution.py:137
  295.2 8.3 %all-to-all-start.3 = ((f32[128,1,128]{2,1,0:T(1,128)}), f32[128,1,128]{2,1,0:T(1,128)S(1)}, u32[]{:S(2)}, u32[]{:S(2)}) async-start(f32[128,1,128]{2,1,0:T(1,128)} %bitcast.10), calls=%async_computation.3 | async-start | bytes 131072 | tf_op jit(solution)/shard_map/all_to_all | solution.py:137
  309.4 18.7 %all-to-all-done.3 = f32[128,1,128]{2,1,0:T(1,128)S(1)} async-done(((f32[128,1,128]{2,1,0:T(1,128)}), f32[128,1,128]{2,1,0:T(1,128)S(1)}, u32[]{:S(2)}, u32[]{:S(2)}) %all-to-all-start.3) | async-done | bytes 65568 | tf_op jit(solution)/shard_map/all_to_all | solution.py:137
  (422 shorter events, 79.9 us)
Async XLA Ops:
  0.8 0.7 copy-start.3
  2.8 289.9 %copy-start.6 = (s32[384]{0:T(512)}, s32[384]{0:T(512)S(1)}, u32[]{:S(2)}) copy-start(s32[384]{0:T(512)S(1)} %eq.75) | copy-start | bytes 4612
  3.3 0.7 copy-start.4
  132.4 5.1 %copy-start = (f32[116,512]{1,0:T(8,128)S(1)}, f32[116,512]{1,0:T(8,128)}, u32[]{:S(2)}) copy-start(f32[116,512]{1,0:T(8,128)} %param.11) | copy-start | bytes 712708
  139.1 47.4 %collective-permute-start = (f32[1,2048]{1,0:T(1,128)S(1)}, f32[1,2048]{1,0:T(1,128)S(1)}, u32[]{:S(2)}, u32[]{:S(2)}) collective-permute-start(f32[1,2048]{1,0:T(1,128)S(1)} %stack_reshape.24), channel_id=1, source_target_pairs={{0,128},{128,256},{256,384},{384,512},{512,640},{640,768},{768,896... | collective-permute-start | bytes 24584 | tf_op jit(solution)/shard_map/ppermute | solution.py:20
  143.5 42.3 %copy-start.5 = (s32[6,116]{1,0:T(8,128)S(1)}, s32[6,116]{1,0:T(8,128)}, u32[]{:S(2)}) copy-start(s32[6,116]{1,0:T(8,128)} %param.14) | copy-start | bytes 8356
  144.2 43.6 %collective-permute-start.1 = (f32[1,2048]{1,0:T(1,128)S(1)}, f32[1,2048]{1,0:T(1,128)S(1)}, u32[]{:S(2)}, u32[]{:S(2)}) collective-permute-start(f32[1,2048]{1,0:T(1,128)S(1)} %stack_reshape.25), channel_id=1, source_target_pairs={{128,0},{256,128},{384,256},{512,384},{640,512},{768,640},{896,768... | collective-permute-start | bytes 24584 | tf_op jit(solution)/shard_map/ppermute | solution.py:23
  151.7 57.8 %all-to-all-start = ((f32[128,1,128]{2,1,0:T(1,128)}), f32[128,1,128]{2,1,0:T(1,128)S(1)}, u32[]{:S(2)}, u32[]{:S(2)}) async-start(f32[128,1,128]{2,1,0:T(1,128)} %bitcast.7), calls=%async_computation | async-start | bytes 131072 | tf_op jit(solution)/shard_map/all_to_all | solution.py:137
  184.7 106.1 %copy-start.9 = (pred[512]{0:T(512)(128)(4,1)}, pred[512]{0:T(512)(128)(4,1)S(1)}, u32[]{:S(2)}) copy-start(pred[512]{0:T(512)(128)(4,1)S(1)} %get-tuple-element.353) | copy-start | bytes 1540
  184.7 106.1 %copy-start.11 = (pred[512]{0:T(512)(128)(4,1)}, pred[512]{0:T(512)(128)(4,1)S(1)}, u32[]{:S(2)}) copy-start(pred[512]{0:T(512)(128)(4,1)S(1)} %get-tuple-element.354) | copy-start | bytes 1540
  184.7 106.1 %copy-start.13 = (pred[512]{0:T(512)(128)(4,1)}, pred[512]{0:T(512)(128)(4,1)S(1)}, u32[]{:S(2)}) copy-start(pred[512]{0:T(512)(128)(4,1)S(1)} %get-tuple-element.351) | copy-start | bytes 1540
  184.7 106.1 %copy-start.15 = (pred[512]{0:T(512)(128)(4,1)}, pred[512]{0:T(512)(128)(4,1)S(1)}, u32[]{:S(2)}) copy-start(pred[512]{0:T(512)(128)(4,1)S(1)} %get-tuple-element.352) | copy-start | bytes 1540
  185.2 0.7 copy-start.8
  185.8 105.0 %copy-start.17 = (f32[116]{0:T(128)}, f32[116]{0:T(128)S(1)}, u32[]{:S(2)}) copy-start(f32[116]{0:T(128)S(1)} %shift-left_convert_fusion) | copy-start | bytes 1396
  186.0 104.8 %copy-start.19 = (pred[512]{0:T(512)(128)(4,1)}, pred[512]{0:T(512)(128)(4,1)S(1)}, u32[]{:S(2)}) copy-start(pred[512]{0:T(512)(128)(4,1)S(1)} %get-tuple-element.349) | copy-start | bytes 1540
  186.0 104.8 %copy-start.21 = (pred[512]{0:T(512)(128)(4,1)}, pred[512]{0:T(512)(128)(4,1)S(1)}, u32[]{:S(2)}) copy-start(pred[512]{0:T(512)(128)(4,1)S(1)} %get-tuple-element.350) | copy-start | bytes 1540
  216.9 30.6 %all-to-all-start.1 = ((f32[128,1,128]{2,1,0:T(1,128)}), f32[128,1,128]{2,1,0:T(1,128)S(1)}, u32[]{:S(2)}, u32[]{:S(2)}) async-start(f32[128,1,128]{2,1,0:T(1,128)} %bitcast.8), calls=%async_computation.1 | async-start | bytes 131072 | tf_op jit(solution)/shard_map/all_to_all | solution.py:137
  224.6 3.1 collective-permute-start.2
  224.6 3.8 %collective-permute-start.3 = (f32[1,2048]{1,0:T(1,128)S(1)}, f32[1,2048]{1,0:T(1,128)S(1)}, u32[]{:S(2)}, u32[]{:S(2)}) collective-permute-start(f32[1,2048]{1,0:T(1,128)S(1)} %stack_reshape.27), channel_id=1, source_target_pairs={{128,0},{256,128},{384,256},{512,384},{640,512},{768,640},{896,768... | collective-permute-start | bytes 24584 | tf_op jit(solution)/shard_map/ppermute | solution.py:23
  254.9 32.1 %all-to-all-start.2 = ((f32[128,1,128]{2,1,0:T(1,128)}), f32[128,1,128]{2,1,0:T(1,128)S(1)}, u32[]{:S(2)}, u32[]{:S(2)}) async-start(f32[128,1,128]{2,1,0:T(1,128)} %bitcast.9), calls=%async_computation.2 | async-start | bytes 131072 | tf_op jit(solution)/shard_map/all_to_all | solution.py:137
  263.5 3.1 collective-permute-start.4
  265.2 2.1 collective-permute-start.5
  295.2 32.9 %all-to-all-start.3 = ((f32[128,1,128]{2,1,0:T(1,128)}), f32[128,1,128]{2,1,0:T(1,128)S(1)}, u32[]{:S(2)}, u32[]{:S(2)}) async-start(f32[128,1,128]{2,1,0:T(1,128)} %bitcast.10), calls=%async_computation.3 | async-start | bytes 131072 | tf_op jit(solution)/shard_map/all_to_all | solution.py:137
  304.9 3.1 collective-permute-start.6
  306.5 2.2 collective-permute-start.7
  331.7 0.8 copy-start.1
  331.8 0.9 copy-start.2
  331.8 0.8 copy-start.16
  331.8 0.8 copy-start.18
  331.8 0.8 copy-start.20
  331.8 0.8 copy-start.22
  332.0 0.7 copy-start.7
  332.0 0.7 copy-start.10
  332.0 0.7 copy-start.12
  332.0 0.7 copy-start.14
where the time goes:
time: 337 us; the launch traced here: 334 us
  local copies, waits for them, and re-layouts  155 us (46%)
  waiting for transfers between devices  79.7 us (24%)
  starting transfers between devices  61.9 us (18%)
  other arithmetic  22.8 us (7%)
  matrix products  11.1 us (3%)
    all_to_all x4, waiting for transfers between devices, laplacian(): lax.all_to_all(departing_faces, 'col', split_axis=0, concat_axis=0, tiled...  76.9 us
    gather x20, local copies, waits for them, and re-layouts, ranked(): first_seen = jnp.searchsorted(sorted_keys, (partner * key_span).reshape(-1))  59.8 us
    all_to_all x4, starting transfers between devices, laplacian(): lax.all_to_all(departing_faces, 'col', split_axis=0, concat_axis=0, tiled...  54.9 us
    gather x11, local copies, waits for them, and re-layouts, per_device(): owner_dev = jnp.searchsorted(offsets, target, side='right') - 1  32.9 us
    sort x2, other arithmetic, ranked(): ordering_index = jnp.argsort(composite)  8.76 us
    scatter x2, local copies, waits for them, and re-layouts, ranked(): position = jnp.zeros_like(composite).at[ordering_index].set(jnp.arange(co...  8.17 us
    gather x8, local copies, waits for them, and re-layouts, laplacian(): ghosts = sources[ghost_rows]  7.37 us
  transfers between devices with their start and end apart: 12, of which 7 were waited for; matrix products, arithmetic and copies ran while one was open for 7% of the time, Pallas kernels for 0%

commit v1 on v0

v1 whole, which is shorter than its diff:
```python
import jax
import jax.numpy as jnp
from jax import lax
from jax.experimental import pallas as pl
from jax.experimental.pallas import tpu as pltpu
from jax.sharding import PartitionSpec as P

MESH = pl.DeviceIdType.MESH
gradient_energy = 0.0625
time_step = 0.0004

LANES = 128
FACES = 6 * LANES
X_RING = 4
SLAB = 32
ROUNDS = 4
BIG = 1e6
f32 = jnp.float32
bf16 = jnp.bfloat16


def iota(shape, dim):
    return lax.broadcasted_iota(jnp.int32, shape, dim)


def onehot(cond):
    return jnp.where(cond, 1.0, 0.0).astype(bf16)


def pieces(v):
    hi = v.astype(bf16)
    rest = v - hi.astype(f32)
    mid = rest.astype(bf16)
    lo = (rest - mid.astype(f32)).astype(bf16)
    return jnp.concatenate([hi, mid, lo], axis=0)


def turned(row):
    return jnp.broadcast_to(row, (LANES, LANES)).T


def layer_parts(ref):
    return [
        ref[0:64, :],
        ref[448:512, :],
        jnp.concatenate([ref[x * 64 : x * 64 + 8, :] for x in range(8)], axis=0),
        jnp.concatenate([ref[x * 64 + 56 : x * 64 + 64, :] for x in range(8)], axis=0),
        ref[pl.ds(0, 64, stride=8), :],
        ref[pl.ds(7, 64, stride=8), :],
    ]


def body(
    n_row, n_col,
    conc_ref, levels_ref, nb_ref, hang_ref, counts_ref,
    next_ref, pot_ref,
    pad_ref, ints_ref, off_ref, field_ref, conc_t_ref, section_ref, inner_ref, zbuf_ref, give_ref, take_ref, local_ref,
    send_ref, recv_ref, send_sem, recv_sem, slab_send_sem, slab_recv_sem,
):
    blocks = conc_ref.shape[0]
    z_ring = n_col // X_RING
    shift = z_ring // 4
    row = lax.axis_index("row")
    col = lax.axis_index("col")
    z = col // X_RING
    x = lax.rem(col, X_RING)
    below = lax.rem(row + n_row - 1, n_row)
    above = lax.rem(row + 1, n_row)

    def peer(dz, dx):
        return lax.rem(z + dz, z_ring) * X_RING + lax.rem(x + dx, X_RING)

    def line(dz, dx):
        return lax.rem(dz + shift, z_ring) * X_RING + dx

    own_line = shift * X_RING
    for r in range(ROUNDS):
        recv_ref[r, own_line : own_line + 1, :] = jnp.zeros((1, LANES), f32)
        recv_ref[r, n_col + SLAB :, :] = jnp.zeros((2 * LANES - n_col - SLAB, LANES), f32)

    barrier = pltpu.get_barrier_semaphore()

    def greet(j, carry):
        pl.semaphore_signal(
            barrier, inc=1, device_id={"col": peer(j // X_RING, lax.rem(j, X_RING))}, device_id_type=MESH
        )
        return carry

    lax.fori_loop(1, n_col, greet, 0)
    for other in (below, above):
        pl.semaphore_signal(barrier, inc=1, device_id={"row": other}, device_id_type=MESH)

    counts = counts_ref[...].astype(f32)
    before = onehot(iota((n_col, n_col), 0) < iota((n_col, n_col), 1))
    partial = jnp.dot(counts.astype(bf16), before, preferred_element_type=f32)
    totals = jnp.sum(counts, axis=1, keepdims=True)
    start = jnp.zeros((1, 1), f32)
    for r in range(n_row):
        off_ref[r : r + 1, :] = partial[r : r + 1, :] + start
        start = start + totals[r : r + 1, :]
    lane = iota((1, LANES), 1)
    mine = lane == col

    def pick(v):
        return jnp.sum(jnp.where(mine, v, 0.0), axis=1, keepdims=True)

    def ranges(r):
        offsets = off_ref[pl.ds(r, 1), :]
        held = counts_ref[pl.ds(r, 1), :].astype(f32)
        return offsets, held

    off_row, held_row = ranges(row)
    off_low, held_low = (pick(v) for v in ranges(below))
    off_high, held_high = (pick(v) for v in ranges(above))
    my_count = pick(held_row)
    row_start = off_row[:, 0:1]
    row_end = row_start + jnp.sum(held_row, axis=1, keepdims=True)
    off_turned = turned(off_row)

    pad_ref[0:blocks, :] = conc_ref[...]
    pad_ref[blocks:, :] = jnp.zeros((LANES - blocks, 512), f32)
    live_rows = iota((LANES, 512), 0).astype(f32) < my_count
    start_field = jnp.where(live_rows, pad_ref[...], 0.0).T
    field_ref[...] = start_field
    conc_t_ref[...] = start_field

    ints_ref[0:8, :] = jnp.full((8, LANES), -1, jnp.int32)
    ints_ref[8:24, :] = jnp.zeros((16, LANES), jnp.int32)
    ints_ref[0:6, 0:blocks] = nb_ref[...]
    ints_ref[8:14, 0:blocks] = hang_ref[...]
    ints_ref[16:17, 0:blocks] = levels_ref[...]
    level = ints_ref[16:17, :]
    scale = jnp.where(level == 0, 1.0, jnp.where(level == 1, 4.0, jnp.where(level == 2, 16.0, 0.0)))
    hanging = jnp.concatenate([ints_ref[8 + f : 9 + f, :] for f in range(6)], axis=1) > 0

    partner_parts, give_parts, take_parts, slab_give, slab_take, low_parts, high_parts = [], [], [], [], [], [], []
    for f in range(6):
        target = ints_ref[f : f + 1, :].astype(f32)
        live = (target >= 0.0) & (lane.astype(f32) < my_count)
        in_row = live & (target >= row_start) & (target < row_end)
        reached = off_turned <= target
        owner = jnp.sum(jnp.where(reached, 1.0, 0.0), axis=0, keepdims=True).astype(jnp.int32) - 1
        first = jnp.max(jnp.where(reached, off_turned, 0.0), axis=0, keepdims=True)
        here = in_row & (owner == col)
        far = in_row & (owner != col)
        low = live & (target >= off_low) & (target < off_low + held_low)
        high = live & (target >= off_high) & (target < off_high + held_high)
        slot = jnp.where(in_row, target - first, jnp.where(low, target - off_low, target - off_high))
        apart = (((owner >> 2) - z + shift) & (z_ring - 1)) * X_RING + ((owner - x) & (X_RING - 1))
        partner_parts.append(jnp.where(far, apart, -1))
        give_key = (lane + f * LANES).astype(f32)
        take_key = slot + float((f ^ 1) * LANES)
        give_parts.append(give_key)
        take_parts.append(take_key)
        slab_give.append(jnp.where(low, give_key, jnp.where(high, give_key + 1024.0, BIG)))
        slab_take.append(jnp.where(low, take_key, jnp.where(high, take_key + 1024.0, BIG)))
        low_parts.append(jnp.where(low, 1.0, 0.0))
        high_parts.append(jnp.where(high, 1.0, 0.0))
        local_ref[f * LANES : (f + 1) * LANES, :] = onehot(
            (iota((LANES, LANES), 0).astype(f32) == slot) & here
        )
    partner = jnp.concatenate(partner_parts, axis=1)
    low_all = jnp.concatenate(low_parts, axis=1)
    high_all = jnp.concatenate(high_parts, axis=1)
    matched = iota((n_col, FACES), 0) == partner
    slab_line = iota((SLAB, FACES), 0)
    slab_id = (slab_line + jnp.where(slab_line >= SLAB // 2, SLAB // 2, 0)).astype(f32)
    n_low = jnp.sum(low_all, axis=1, keepdims=True)
    for ref, stride, keys, slab_keys in (
        (give_ref, n_col + SLAB, give_parts, slab_give),
        (take_ref, 2 * LANES, take_parts, slab_take),
    ):
        key = jnp.concatenate(keys, axis=1)
        least = jnp.min(jnp.where(matched, key, BIG), axis=1, keepdims=True)
        ref[0:n_col, :] = onehot(matched & (key == least))
        ref[stride : stride + n_col, :] = onehot(matched & (key != least))
        slab_key = jnp.concatenate(slab_keys, axis=1)
        smaller = jnp.zeros((1, FACES), f32)
        for f in range(6):
            smaller = smaller + jnp.sum(
                jnp.where(turned(slab_keys[f])[:, 0:1] < slab_key, 1.0, 0.0), axis=0, keepdims=True
            )
        place = jnp.where(low_all > 0.0, smaller, jnp.where(high_all > 0.0, smaller - n_low + SLAB, -1.0))
        ref[n_col : n_col + SLAB, :] = onehot(slab_id == place)
        ref[stride + n_col : stride + n_col + SLAB, :] = onehot(slab_id + SLAB // 2 == place)
    take_ref[n_col + SLAB : 2 * LANES, :] = jnp.zeros((2 * LANES - n_col - SLAB, FACES), bf16)
    take_ref[2 * LANES + n_col + SLAB :, :] = jnp.zeros((2 * LANES - n_col - SLAB, FACES), bf16)
    zbuf_ref[...] = jnp.zeros((512, LANES), f32)

    pl.semaphore_wait(barrier, n_col + 1)

    def start_copy(r, dz, dx):
        pltpu.make_async_remote_copy(
            src_ref=send_ref.at[r, pl.ds(line(dz, dx), 1)],
            dst_ref=recv_ref.at[r, pl.ds(line(z_ring - dz, lax.rem(X_RING - dx, X_RING)), 1)],
            send_sem=send_sem.at[r],
            recv_sem=recv_sem.at[r],
            device_id={"col": peer(dz, dx)},
            device_id_type=MESH,
        ).start()

    def slab_copy(r, side, other):
        half = SLAB // 2
        return pltpu.make_async_remote_copy(
            src_ref=send_ref.at[r, pl.ds(n_col + side * half, half)],
            dst_ref=recv_ref.at[r, pl.ds(n_col + (1 - side) * half, half)],
            send_sem=slab_send_sem.at[r, side],
            recv_sem=slab_recv_sem.at[r, side],
            device_id={"row": other},
            device_id_type=MESH,
        )

    def all_lines(r):
        return pltpu.make_async_remote_copy(
            src_ref=send_ref.at[r, pl.ds(0, n_col - 1)],
            dst_ref=recv_ref.at[r, pl.ds(0, n_col - 1)],
            send_sem=send_sem.at[r],
            recv_sem=recv_sem.at[r],
            device_id={"col": peer(1, 0)},
            device_id_type=MESH,
        )

    def laplacian(r):
        layers = layer_parts(field_ref)
        cut = pieces(jnp.concatenate(layers, axis=1))
        given = lax.dot_general(give_ref[...], cut, (((1,), (1,)), ((), ())), preferred_element_type=f32)
        given = given[:, 0:64] + (given[:, 64:128] + given[:, 128:192])
        lines = n_col + SLAB
        send_ref[r, :, 0:64] = given[0:lines]
        send_ref[r, :, 64:128] = given[lines : 2 * lines]
        for dx in range(X_RING):
            start_copy(r, z_ring // 2, dx)

        def outward(i, carry):
            near = z_ring // 2 - i
            for dx in range(X_RING):
                start_copy(r, near, dx)
                start_copy(r, z_ring - near, dx)
            return carry

        lax.fori_loop(1, z_ring // 2, outward, 0)
        for dx in range(1, X_RING):
            start_copy(r, 0, dx)
        slabs = [slab_copy(r, 0, below), slab_copy(r, 1, above)]
        for copy in slabs:
            copy.start()

        cells = field_ref[...]
        cube = cells.reshape(8, 8, 8, LANES)
        zero_x = jnp.zeros((1, 8, 8, LANES), f32)
        zero_y = jnp.zeros((8, 1, 8, LANES), f32)
        summed = jnp.concatenate([zero_x, cube[:7]], axis=0) + jnp.concatenate([cube[1:], zero_x], axis=0)
        summed = summed + jnp.concatenate([zero_y, cube[:, :7]], axis=1)
        summed = summed + jnp.concatenate([cube[:, 1:], zero_y], axis=1)
        columns = cells.reshape(64, 8, LANES)
        z_at = iota((64, 8, LANES), 1)
        prev_z = jnp.where(z_at > 0, pltpu.roll(columns, 1, 1), 0.0)
        next_z = jnp.where(z_at < 7, pltpu.roll(columns, 7, 1), 0.0)
        inner_ref[...] = summed.reshape(512, LANES) + (prev_z + next_z).reshape(512, LANES) - 6.0 * cells
        near_ghosts = []
        for f in range(6):
            g = f ^ 1
            part = jnp.dot(
                cut[:, g * LANES : (g + 1) * LANES],
                local_ref[f * LANES : (f + 1) * LANES, :],
                preferred_element_type=f32,
            )
            near_ghosts.append(part[0:64] + (part[64:128] + part[128:192]))
        ghosts = jnp.concatenate(near_ghosts, axis=1)

        all_lines(r).wait_recv()
        for copy in slabs:
            copy.wait_recv()
        taken = recv_ref[r].T
        taken = pieces(jnp.concatenate([taken[0:64], taken[64:128]], axis=1))
        taken = jnp.dot(taken, take_ref[...], preferred_element_type=f32)
        ghosts = ghosts + (taken[0:64] + (taken[64:128] + taken[128:192]))
        pairs = ghosts.reshape(4, 2, 8, FACES)
        pairs = pairs[:, 0] + pairs[:, 1]
        even = iota((4, 8, FACES), 1) % 2 == 0
        pairs = 0.25 * (pairs + jnp.where(even, pltpu.roll(pairs, 7, 1), pltpu.roll(pairs, 1, 1)))
        coarse = jnp.broadcast_to(pairs[:, None], (4, 2, 8, FACES)).reshape(64, FACES)
        ghosts = jnp.where(hanging, coarse, ghosts)

        sides = [ghosts[:, f * LANES : (f + 1) * LANES] for f in range(6)]
        inner_ref[0:64, :] += sides[0]
        inner_ref[448:512, :] += sides[1]
        for i in range(8):
            inner_ref[i * 64 : i * 64 + 8, :] += sides[2][i * 8 : i * 8 + 8]
            inner_ref[i * 64 + 56 : i * 64 + 64, :] += sides[3][i * 8 : i * 8 + 8]
        zbuf_ref[pl.ds(0, 64, stride=8), :] = sides[4]
        zbuf_ref[pl.ds(7, 64, stride=8), :] = sides[5]
        return (inner_ref[...] + zbuf_ref[...]) * scale

    def potential(v, lap):
        return v * v * v - v - gradient_energy * lap

    field_ref[...] = potential(conc_t_ref[...], laplacian(0))
    section = conc_t_ref[...] + time_step * laplacian(1)
    section_ref[...] = section
    field_ref[...] = section
    second = potential(section_ref[...], laplacian(2))
    field_ref[...] = second
    finished = 0.5 * (conc_t_ref[...] + section_ref[...] + time_step * laplacian(3))
    pot_ref[...] = field_ref[...].T[0:blocks]
    next_ref[...] = finished.T[0:blocks]
    for r in range(ROUNDS):
        all_lines(r).wait_send()
        slab_copy(r, 0, below).wait_send()
        slab_copy(r, 1, above).wait_send()


def per_device(n_row, n_col):
    def run(conc, levels, neighbours, hanging, block_counts):
        blocks = conc.shape[0]
        vmem = pl.BlockSpec(memory_space=pltpu.VMEM)
        lines = n_col + SLAB
        whole = pltpu.VMEM((512, LANES), f32)

        def kernel(*refs):
            body(n_row, n_col, *refs)

        return pl.pallas_call(
            kernel,
            out_shape=[jax.ShapeDtypeStruct((blocks, 512), f32)] * 2,
            in_specs=[vmem] * 5,
            out_specs=[vmem] * 2,
            scratch_shapes=[
                pltpu.VMEM((LANES, 512), f32),
                pltpu.VMEM((24, LANES), jnp.int32),
                pltpu.VMEM((n_row, n_col), f32),
                whole, whole, whole, whole, whole,
                pltpu.VMEM((2 * lines, FACES), bf16),
                pltpu.VMEM((4 * LANES, FACES), bf16),
                pltpu.VMEM((FACES, LANES), bf16),
                pltpu.VMEM((ROUNDS, lines, LANES), f32),
                pltpu.VMEM((ROUNDS, 2 * LANES, LANES), f32),
                pltpu.SemaphoreType.DMA((ROUNDS,)),
                pltpu.SemaphoreType.DMA((ROUNDS,)),
                pltpu.SemaphoreType.DMA((ROUNDS, 2)),
                pltpu.SemaphoreType.DMA((ROUNDS, 2)),
            ],
            compiler_params=pltpu.CompilerParams(
                collective_id=0, has_side_effects=True, vmem_limit_bytes=32 * 1024 * 1024
            ),
        )(conc, levels.reshape(1, blocks), neighbours, hanging, block_counts.reshape(n_row, n_col))

    return run


def solution(mesh):
    return jax.shard_map(
        per_device(mesh.shape["row"], mesh.shape["col"]),
        mesh=mesh,
        in_specs=(
            P(("row", "col"), None),
            P(("row", "col")),
            P(None, ("row", "col")),
            P(None, ("row", "col")),
            P(),
        ),
        out_specs=(P(("row", "col"), None), P(("row", "col"), None)),
        check_vma=False,
    )
```

time: 337 us -> 94.8 us (0.28)
  local copies, waits for them, and re-layouts: 155 us -> 5.04 us
  Pallas kernels: 0 us -> 88.8 us
  waiting for transfers between devices: 79.7 us -> 0 us
  starting transfers between devices: 61.9 us -> 0 us
  other arithmetic: 22.8 us -> 0 us
  matrix products: 11.1 us -> 0 us
    gather x55 -> x0, local copies, waits for them, and re-layouts: 117 us -> none  [the longest x20 59.8 us: ranked(): first_seen = jnp.searchsorted(sorted_keys, (partner * key_span).reshape(-1))]
    pallas_call x0 -> x1, Pallas kernels: none -> 88.8 us  [run(): pl.pallas_call(kernel, out_shape=[jax.ShapeDtypeStruct((blocks, 512), f32...]
    all_to_all x4 -> x0, waiting for transfers between devices: 76.9 us -> none  [laplacian(): lax.all_to_all(departing_faces, 'col', split_axis=0, concat_axis=0, tiled...]
    all_to_all x4 -> x0, starting transfers between devices: 54.9 us -> none  [laplacian(): lax.all_to_all(departing_faces, 'col', split_axis=0, concat_axis=0, tiled...]
    scatter x5 -> x0, local copies, waits for them, and re-layouts: 20.6 us -> none  [the longest x2 8.17 us: ranked(): position = jnp.zeros_like(composite).at[ordering_index].set(jnp.arange(co...]
    dot_general x12 -> x0, matrix products: 11.1 us -> none  [the longest x4 5.73 us: laplacian(): beyond = jnp.dot(ghosts, spreading, precision=lax.Precision.HIGHEST)]
    sort x2 -> x0, other arithmetic: 8.76 us -> none  [ranked(): ordering_index = jnp.argsort(composite)]
    ppermute x8 -> x0, starting transfers between devices: 6.98 us -> none  [the longest x4 3.68 us: with_halo(): lax.ppermute(lax.slice_in_dim(block, 0, width, axis=dim), axis, backward)]
  transfers between devices with their start and end apart: 12 -> 0, of which waited for: 7 -> 0; matrix products, arithmetic and copies ran while one was open for 7% -> 0% of each run, Pallas kernels for 0% -> 0%
where the time goes in v1:
time: 94.8 us; the launch traced here: 94.5 us
  Pallas kernels  88.8 us (94%)
  local copies, waits for them, and re-layouts  5.04 us (5%)
    pallas_call x1, Pallas kernels, run(): pl.pallas_call(kernel, out_shape=[jax.ShapeDtypeStruct((blocks, 512), f32...  88.8 us
    unnamed x12, local copies, waits for them, and re-layouts  5.04 us

profile of v1, /device:TPU:24, one launch (start us, length us, event | category | flops | bytes accessed | tf_op | source)
XLA Modules:
  0.0 94.5 jit_solution(7306608230451611103)
XLA Ops:
  0.6 0.0 copy-start.4
  0.6 0.6 copy-done.4
  1.3 0.0 copy-start
  1.3 0.9 copy-done
  2.2 0.0 copy-start.1
  2.2 0.7 copy-done.1
  2.9 0.0 copy-start.2
  2.9 0.7 copy-done.2
  3.6 0.0 copy-start.3
  3.6 0.7 copy-done.3
  4.3 88.8 %shard_map.68 = (f32[116,512]{1,0:T(8,128)S(1)}, f32[116,512]{1,0:T(8,128)S(1)}) custom-call(f32[116,512]{1,0:T(8,128)S(1)} %copy-done, s32[1,116]{1,0:T(1,128)S(1)} %bitcast.3, s32[6,116]{1,0:T(8,128)S(1)} %copy-done.1, s32[6,116]{1,0:T(8,128)S(1)} %copy-done.2, s32[8,128]{1,0:T(8,128)S(1)} %bitcast.2), custom_call_target="tpu_custom_call" | custom-call | tf_op jit(solution)/shard_map/pallas_call | solution.py:323
  93.1 0.7 copy.9
  93.8 0.7 copy.10
Async XLA Ops:
  0.6 0.7 copy-start.4
  1.3 0.9 copy-start
  2.2 0.7 copy-start.1
  2.9 0.7 copy-start.2
  3.6 0.7 copy-start.3

commit v2 on v1

--- a/solution.py
+++ b/solution.py
@@ -14,6 +14,7 @@
 X_RING = 4
 SLAB = 32
 ROUNDS = 4
+OUTER_FIRST = (2, 1, 3, 0)
 BIG = 1e6
 f32 = jnp.float32
 bf16 = jnp.bfloat16
@@ -54,12 +55,14 @@
     n_row, n_col,
     conc_ref, levels_ref, nb_ref, hang_ref, counts_ref,
     next_ref, pot_ref,
-    pad_ref, ints_ref, off_ref, field_ref, conc_t_ref, section_ref, inner_ref, zbuf_ref, give_ref, take_ref, local_ref,
+    conc_in, pad_ref, levels_in, nb_in, hang_in, counts_in, load_sem,
+    ints_ref, off_ref, field_ref, conc_t_ref, section_ref, inner_ref, zbuf_ref, give_ref, take_ref, local_ref,
     send_ref, recv_ref, send_sem, recv_sem, slab_send_sem, slab_recv_sem,
 ):
     blocks = conc_ref.shape[0]
     z_ring = n_col // X_RING
     shift = z_ring // 4
+    half = n_col // 2
     row = lax.axis_index("row")
     col = lax.axis_index("col")
     z = col // X_RING
@@ -76,21 +79,45 @@
     own_line = shift * X_RING
     for r in range(ROUNDS):
         recv_ref[r, own_line : own_line + 1, :] = jnp.zeros((1, LANES), f32)
-        recv_ref[r, n_col + SLAB :, :] = jnp.zeros((2 * LANES - n_col - SLAB, LANES), f32)
 
     barrier = pltpu.get_barrier_semaphore()
 
-    def greet(j, carry):
-        pl.semaphore_signal(
-            barrier, inc=1, device_id={"col": peer(j // X_RING, lax.rem(j, X_RING))}, device_id_type=MESH
-        )
+    def greet(dz, dx):
+        pl.semaphore_signal(barrier, inc=1, device_id={"col": peer(dz, dx)}, device_id_type=MESH)
+
+    def greet_pair(i, carry):
+        away = z_ring // 2 - i
+        for dx in OUTER_FIRST:
+            greet(away, dx)
+            greet(z_ring - away, dx)
         return carry
 
-    lax.fori_loop(1, n_col, greet, 0)
+    for dx in OUTER_FIRST:
+        greet(z_ring // 2, dx)
+    lax.fori_loop(1, z_ring // 2, greet_pair, 0)
+    for dx in range(1, X_RING):
+        greet(0, dx)
     for other in (below, above):
         pl.semaphore_signal(barrier, inc=1, device_id={"row": other}, device_id_type=MESH)
 
-    counts = counts_ref[...].astype(f32)
+    loads = [
+        pltpu.make_async_copy(src, dst, load_sem.at[i])
+        for i, (src, dst) in enumerate(
+            (
+                (counts_ref, counts_in),
+                (nb_ref, nb_in),
+                (conc_ref, conc_in),
+                (hang_ref, hang_in),
+                (levels_ref, levels_in),
+            )
+        )
+    ]
+    for load in loads:
+        load.start()
+    for load in loads:
+        load.wait()
+
+    counts = counts_in[...].astype(f32)
     before = onehot(iota((n_col, n_col), 0) < iota((n_col, n_col), 1))
     partial = jnp.dot(counts.astype(bf16), before, preferred_element_type=f32)
     totals = jnp.sum(counts, axis=1, keepdims=True)
@@ -106,7 +133,7 @@
 
     def ranges(r):
         offsets = off_ref[pl.ds(r, 1), :]
-        held = counts_ref[pl.ds(r, 1), :].astype(f32)
+        held = counts_in[pl.ds(r, 1), :].astype(f32)
         return offsets, held
 
     off_row, held_row = ranges(row)
@@ -117,7 +144,7 @@
     row_end = row_start + jnp.sum(held_row, axis=1, keepdims=True)
     off_turned = turned(off_row)
 
-    pad_ref[0:blocks, :] = conc_ref[...]
+    pad_ref[0:blocks, :] = conc_in[...]
     pad_ref[blocks:, :] = jnp.zeros((LANES - blocks, 512), f32)
     live_rows = iota((LANES, 512), 0).astype(f32) < my_count
     start_field = jnp.where(live_rows, pad_ref[...], 0.0).T
@@ -126,9 +153,9 @@
 
     ints_ref[0:8, :] = jnp.full((8, LANES), -1, jnp.int32)
     ints_ref[8:24, :] = jnp.zeros((16, LANES), jnp.int32)
-    ints_ref[0:6, 0:blocks] = nb_ref[...]
-    ints_ref[8:14, 0:blocks] = hang_ref[...]
-    ints_ref[16:17, 0:blocks] = levels_ref[...]
+    ints_ref[0:6, 0:blocks] = nb_in[...]
+    ints_ref[8:14, 0:blocks] = hang_in[...]
+    ints_ref[16:17, 0:blocks] = levels_in[...]
     level = ints_ref[16:17, :]
     scale = jnp.where(level == 0, 1.0, jnp.where(level == 1, 4.0, jnp.where(level == 2, 16.0, 0.0)))
     hanging = jnp.concatenate([ints_ref[8 + f : 9 + f, :] for f in range(6)], axis=1) > 0
@@ -166,14 +193,12 @@
     slab_line = iota((SLAB, FACES), 0)
     slab_id = (slab_line + jnp.where(slab_line >= SLAB // 2, SLAB // 2, 0)).astype(f32)
     n_low = jnp.sum(low_all, axis=1, keepdims=True)
-    for ref, stride, keys, slab_keys in (
-        (give_ref, n_col + SLAB, give_parts, slab_give),
-        (take_ref, 2 * LANES, take_parts, slab_take),
-    ):
+    for ref, keys, slab_keys in ((give_ref, give_parts, slab_give), (take_ref, take_parts, slab_take)):
         key = jnp.concatenate(keys, axis=1)
         least = jnp.min(jnp.where(matched, key, BIG), axis=1, keepdims=True)
-        ref[0:n_col, :] = onehot(matched & (key == least))
-        ref[stride : stride + n_col, :] = onehot(matched & (key != least))
+        for i, lines in enumerate((onehot(matched & (key == least)), onehot(matched & (key != least)))):
+            ref[i * half : (i + 1) * half, :] = lines[half:]
+            ref[n_col + i * half : n_col + (i + 1) * half, :] = lines[:half]
         slab_key = jnp.concatenate(slab_keys, axis=1)
         smaller = jnp.zeros((1, FACES), f32)
         for f in range(6):
@@ -181,66 +206,87 @@
                 jnp.where(turned(slab_keys[f])[:, 0:1] < slab_key, 1.0, 0.0), axis=0, keepdims=True
             )
         place = jnp.where(low_all > 0.0, smaller, jnp.where(high_all > 0.0, smaller - n_low + SLAB, -1.0))
-        ref[n_col : n_col + SLAB, :] = onehot(slab_id == place)
-        ref[stride + n_col : stride + n_col + SLAB, :] = onehot(slab_id + SLAB // 2 == place)
-    take_ref[n_col + SLAB : 2 * LANES, :] = jnp.zeros((2 * LANES - n_col - SLAB, FACES), bf16)
-    take_ref[2 * LANES + n_col + SLAB :, :] = jnp.zeros((2 * LANES - n_col - SLAB, FACES), bf16)
+        ref[2 * n_col : 2 * n_col + SLAB, :] = onehot(slab_id == place)
+        ref[2 * n_col + SLAB : 2 * n_col + 2 * SLAB, :] = onehot(slab_id + SLAB // 2 == place)
     zbuf_ref[...] = jnp.zeros((512, LANES), f32)
 
     pl.semaphore_wait(barrier, n_col + 1)
 
-    def start_copy(r, dz, dx):
+    def start_copy(r, dz, dx, far):
         pltpu.make_async_remote_copy(
             src_ref=send_ref.at[r, pl.ds(line(dz, dx), 1)],
             dst_ref=recv_ref.at[r, pl.ds(line(z_ring - dz, lax.rem(X_RING - dx, X_RING)), 1)],
             send_sem=send_sem.at[r],
-            recv_sem=recv_sem.at[r],
+            recv_sem=recv_sem.at[r, far],
             device_id={"col": peer(dz, dx)},
             device_id_type=MESH,
         ).start()
 
     def slab_copy(r, side, other):
-        half = SLAB // 2
+        part = SLAB // 2
         return pltpu.make_async_remote_copy(
-            src_ref=send_ref.at[r, pl.ds(n_col + side * half, half)],
-            dst_ref=recv_ref.at[r, pl.ds(n_col + (1 - side) * half, half)],
+            src_ref=send_ref.at[r, pl.ds(n_col + side * part, part)],
+            dst_ref=recv_ref.at[r, pl.ds(n_col + (1 - side) * part, part)],
             send_sem=slab_send_sem.at[r, side],
             recv_sem=slab_recv_sem.at[r, side],
             device_id={"row": other},
             device_id_type=MESH,
         )
 
-    def all_lines(r):
+    def lines_in(r, far, count):
         return pltpu.make_async_remote_copy(
-            src_ref=send_ref.at[r, pl.ds(0, n_col - 1)],
-            dst_ref=recv_ref.at[r, pl.ds(0, n_col - 1)],
+            src_ref=send_ref.at[r, pl.ds(0, count)],
+            dst_ref=recv_ref.at[r, pl.ds(0, count)],
             send_sem=send_sem.at[r],
-            recv_sem=recv_sem.at[r],
+            recv_sem=recv_sem.at[r, far],
             device_id={"col": peer(1, 0)},
             device_id_type=MESH,
         )
+
+    def summed(v):
+        return v[0:64] + (v[64:128] + v[128:192])
+
+    def by_cell(lines):
+        turned_lines = lines.T
+        return jnp.concatenate([turned_lines[0:64], turned_lines[64:128]], axis=1)
 
     def laplacian(r):
         layers = layer_parts(field_ref)
         cut = pieces(jnp.concatenate(layers, axis=1))
-        given = lax.dot_general(give_ref[...], cut, (((1,), (1,)), ((), ())), preferred_element_type=f32)
-        given = given[:, 0:64] + (given[:, 64:128] + given[:, 128:192])
-        lines = n_col + SLAB
-        send_ref[r, :, 0:64] = given[0:lines]
-        send_ref[r, :, 64:128] = given[lines : 2 * lines]
-        for dx in range(X_RING):
-            start_copy(r, z_ring // 2, dx)
-
-        def outward(i, carry):
-            near = z_ring // 2 - i
-            for dx in range(X_RING):
-                start_copy(r, near, dx)
-                start_copy(r, z_ring - near, dx)
-            return carry
-
-        lax.fori_loop(1, z_ring // 2, outward, 0)
+
+        def give(first, last):
+            given = lax.dot_general(
+                give_ref[first:last, :], cut, (((1,), (1,)), ((), ())), preferred_element_type=f32
+            )
+            return given[:, 0:64] + (given[:, 64:128] + given[:, 128:192])
+
+        def outward(far):
+            def step(away, carry):
+                for dx in OUTER_FIRST:
+                    start_copy(r, away, dx, far)
+                    start_copy(r, z_ring - away, dx, far)
+                return carry
+
+            return lambda i, carry: step(z_ring // 2 - i, carry)
+
+        given = give(0, n_col)
+        send_ref[r, half:n_col, 0:64] = given[0:half]
+        send_ref[r, half:n_col, 64:128] = given[half:n_col]
+        for dx in OUTER_FIRST:
+            start_copy(r, z_ring // 2, dx, 1)
+        lax.fori_loop(1, z_ring // 2 - shift, outward(1), 0)
+        for dx in OUTER_FIRST:
+            start_copy(r, shift, dx, 0)
+        given = give(n_col, 2 * n_col + 2 * SLAB)
+        send_ref[r, 0:half, 0:64] = given[0:half]
+        send_ref[r, 0:half, 64:128] = given[half:n_col]
+        send_ref[r, n_col:, 0:64] = given[n_col : n_col + SLAB]
+        send_ref[r, n_col:, 64:128] = given[n_col + SLAB :]
+        for dx in OUTER_FIRST:
+            start_copy(r, z_ring - shift, dx, 1)
+        lax.fori_loop(z_ring // 2 - shift + 1, z_ring // 2, outward(0), 0)
         for dx in range(1, X_RING):
-            start_copy(r, 0, dx)
+            start_copy(r, 0, dx, 0)
         slabs = [slab_copy(r, 0, below), slab_copy(r, 1, above)]
         for copy in slabs:
             copy.start()
@@ -249,14 +295,14 @@
         cube = cells.reshape(8, 8, 8, LANES)
         zero_x = jnp.zeros((1, 8, 8, LANES), f32)
         zero_y = jnp.zeros((8, 1, 8, LANES), f32)
-        summed = jnp.concatenate([zero_x, cube[:7]], axis=0) + jnp.concatenate([cube[1:], zero_x], axis=0)
-        summed = summed + jnp.concatenate([zero_y, cube[:, :7]], axis=1)
-        summed = summed + jnp.concatenate([cube[:, 1:], zero_y], axis=1)
+        steps = jnp.concatenate([zero_x, cube[:7]], axis=0) + jnp.concatenate([cube[1:], zero_x], axis=0)
+        steps = steps + jnp.concatenate([zero_y, cube[:, :7]], axis=1)
+        steps = steps + jnp.concatenate([cube[:, 1:], zero_y], axis=1)
         columns = cells.reshape(64, 8, LANES)
         z_at = iota((64, 8, LANES), 1)
         prev_z = jnp.where(z_at > 0, pltpu.roll(columns, 1, 1), 0.0)
         next_z = jnp.where(z_at < 7, pltpu.roll(columns, 7, 1), 0.0)
-        inner_ref[...] = summed.reshape(512, LANES) + (prev_z + next_z).reshape(512, LANES) - 6.0 * cells
+        inner_ref[...] = steps.reshape(512, LANES) + (prev_z + next_z).reshape(512, LANES) - 6.0 * cells
         near_ghosts = []
         for f in range(6):
             g = f ^ 1
@@ -265,16 +311,24 @@
                 local_ref[f * LANES : (f + 1) * LANES, :],
                 preferred_element_type=f32,
             )
-            near_ghosts.append(part[0:64] + (part[64:128] + part[128:192]))
+            near_ghosts.append(summed(part))
         ghosts = jnp.concatenate(near_ghosts, axis=1)
 
-        all_lines(r).wait_recv()
+        if r == ROUNDS - 1:
+            pot_ref[...] = cells.T[0:blocks]
+
+        lines_in(r, 0, half - 1).wait_recv()
         for copy in slabs:
             copy.wait_recv()
-        taken = recv_ref[r].T
-        taken = pieces(jnp.concatenate([taken[0:64], taken[64:128]], axis=1))
-        taken = jnp.dot(taken, take_ref[...], preferred_element_type=f32)
-        ghosts = ghosts + (taken[0:64] + (taken[64:128] + taken[128:192]))
+        taken = jnp.concatenate([by_cell(recv_ref[r, 0:half, :]), by_cell(recv_ref[r, n_col:, :])], axis=1)
+        ghosts = ghosts + summed(
+            jnp.dot(pieces(taken), take_ref[n_col:, :], preferred_element_type=f32)
+        )
+        lines_in(r, 1, half).wait_recv()
+        taken = by_cell(recv_ref[r, half:n_col, :])
+        ghosts = ghosts + summed(
+            jnp.dot(pieces(taken), take_ref[0:n_col, :], preferred_element_type=f32)
+        )
         pairs = ghosts.reshape(4, 2, 8, FACES)
         pairs = pairs[:, 0] + pairs[:, 1]
         even = iota((4, 8, FACES), 1) % 2 == 0
@@ -302,10 +356,9 @@
     second = potential(section_ref[...], laplacian(2))
     field_ref[...] = second
     finished = 0.5 * (conc_t_ref[...] + section_ref[...] + time_step * laplacian(3))
-    pot_ref[...] = field_ref[...].T[0:blocks]
     next_ref[...] = finished.T[0:blocks]
     for r in range(ROUNDS):
-        all_lines(r).wait_send()
+        lines_in(r, 0, n_col - 1).wait_send()
         slab_copy(r, 0, below).wait_send()
         slab_copy(r, 1, above).wait_send()
 
@@ -322,28 +375,39 @@
 
         return pl.pallas_call(
             kernel,
-            out_shape=[jax.ShapeDtypeStruct((blocks, 512), f32)] * 2,
-            in_specs=[vmem] * 5,
+            out_shape=[pltpu.VMEM((blocks, 512), f32)] * 2,
+            in_specs=[pl.BlockSpec(memory_space=pltpu.HBM)] * 5,
             out_specs=[vmem] * 2,
             scratch_shapes=[
+                pltpu.VMEM((blocks, 512), f32),
                 pltpu.VMEM((LANES, 512), f32),
+                pltpu.VMEM((1, blocks), jnp.int32),
+                pltpu.VMEM((6, blocks), jnp.int32),
+                pltpu.VMEM((6, blocks), jnp.int32),
+                pltpu.VMEM((n_row, n_col), jnp.int32),
+                pltpu.SemaphoreType.DMA((5,)),
                 pltpu.VMEM((24, LANES), jnp.int32),
                 pltpu.VMEM((n_row, n_col), f32),
                 whole, whole, whole, whole, whole,
                 pltpu.VMEM((2 * lines, FACES), bf16),
-                pltpu.VMEM((4 * LANES, FACES), bf16),
+                pltpu.VMEM((2 * lines, FACES), bf16),
                 pltpu.VMEM((FACES, LANES), bf16),
                 pltpu.VMEM((ROUNDS, lines, LANES), f32),
-                pltpu.VMEM((ROUNDS, 2 * LANES, LANES), f32),
+                pltpu.VMEM((ROUNDS, lines, LANES), f32),
                 pltpu.SemaphoreType.DMA((ROUNDS,)),
-                pltpu.SemaphoreType.DMA((ROUNDS,)),
+                pltpu.SemaphoreType.DMA((ROUNDS, 2)),
                 pltpu.SemaphoreType.DMA((ROUNDS, 2)),
                 pltpu.SemaphoreType.DMA((ROUNDS, 2)),
             ],
             compiler_params=pltpu.CompilerParams(
                 collective_id=0, has_side_effects=True, vmem_limit_bytes=32 * 1024 * 1024
             ),
-        )(conc, levels.reshape(1, blocks), neighbours, hanging, block_counts.reshape(n_row, n_col))
+        )(
+            *(
+                pltpu.with_memory_space_constraint(v, pltpu.HBM)
+                for v in (conc, levels.reshape(1, blocks), neighbours, hanging, block_counts.reshape(n_row, n_col))
+            )
+        )
 
     return run
 

time: 94.8 us -> 88.9 us (0.938)
  local copies, waits for them, and re-layouts: 5.04 us -> 1.39 us
  Pallas kernels: 88.8 us -> 86.7 us
    unnamed x12 -> x2, local copies, waits for them, and re-layouts: 5.04 us -> 1.39 us
    pallas_call x1, Pallas kernels: 88.8 us -> 86.7 us  [run(): pl.pallas_call(kernel, out_shape=[pltpu.VMEM((blocks, 512), f32)] * 2, in...]
where the time goes in v2:
time: 88.9 us; the launch traced here: 88.7 us
  Pallas kernels  86.7 us (98%)
  local copies, waits for them, and re-layouts  1.39 us (2%)
    pallas_call x1, Pallas kernels, run(): pl.pallas_call(kernel, out_shape=[pltpu.VMEM((blocks, 512), f32)] * 2, in...  86.7 us

profile of v2, /device:TPU:24, one launch (start us, length us, event | category | flops | bytes accessed | tf_op | source)
XLA Modules:
  0.0 88.7 jit_solution(10335848203863174753)
XLA Ops:
  0.6 86.7 %shard_map.68 = (f32[116,512]{1,0:T(8,128)S(1)}, f32[116,512]{1,0:T(8,128)S(1)}) custom-call(f32[116,512]{1,0:T(8,128)} %refs_0_.1, s32[1,116]{1,0:T(1,128)} %bitcast.3, s32[6,116]{1,0:T(8,128)} %refs_2_.1, s32[6,116]{1,0:T(8,128)} %refs_3_.1, s32[8,128]{1,0:T(8,128)} %bitcast.2), custom_call_target="tpu_custom_call" | custom-call | tf_op jit(solution)/shard_map/pallas_call | solution.py:376
  87.3 0.7 copy.9
  88.0 0.7 copy.10

commit v3 on v2

--- a/solution.py
+++ b/solution.py
@@ -57,7 +57,7 @@
     next_ref, pot_ref,
     conc_in, pad_ref, levels_in, nb_in, hang_in, counts_in, load_sem,
     ints_ref, off_ref, field_ref, conc_t_ref, section_ref, inner_ref, zbuf_ref, give_ref, take_ref, local_ref,
-    send_ref, recv_ref, send_sem, recv_sem, slab_send_sem, slab_recv_sem,
+    send_ref, recv_ref, mid_ref, send_sem, recv_sem, slab_send_sem, slab_recv_sem, mid_send_sem, mid_recv_sem,
 ):
     blocks = conc_ref.shape[0]
     z_ring = n_col // X_RING
@@ -86,15 +86,13 @@
         pl.semaphore_signal(barrier, inc=1, device_id={"col": peer(dz, dx)}, device_id_type=MESH)
 
     def greet_pair(i, carry):
-        away = z_ring // 2 - i
+        away = shift + 1 - i
         for dx in OUTER_FIRST:
             greet(away, dx)
             greet(z_ring - away, dx)
         return carry
 
-    for dx in OUTER_FIRST:
-        greet(z_ring // 2, dx)
-    lax.fori_loop(1, z_ring // 2, greet_pair, 0)
+    lax.fori_loop(1, shift + 1, greet_pair, 0)
     for dx in range(1, X_RING):
         greet(0, dx)
     for other in (below, above):
@@ -210,17 +208,76 @@
         ref[2 * n_col + SLAB : 2 * n_col + 2 * SLAB, :] = onehot(slab_id + SLAB // 2 == place)
     zbuf_ref[...] = jnp.zeros((512, LANES), f32)
 
-    pl.semaphore_wait(barrier, n_col + 1)
-
-    def start_copy(r, dz, dx, far):
+    pl.semaphore_wait(barrier, (2 * shift + 1) * X_RING + 1)
+
+    def start_copy(r, dz, dx, far, left=None):
         pltpu.make_async_remote_copy(
-            src_ref=send_ref.at[r, pl.ds(line(dz, dx), 1)],
+            src_ref=(send_ref.at[r] if left is None else mid_ref).at[pl.ds(line(dz, dx), 1)],
             dst_ref=recv_ref.at[r, pl.ds(line(z_ring - dz, lax.rem(X_RING - dx, X_RING)), 1)],
             send_sem=send_sem.at[r],
             recv_sem=recv_sem.at[r, far],
-            device_id={"col": peer(dz, dx)},
+            device_id={"col": peer(dz if left is None else left, dx)},
             device_id_type=MESH,
         ).start()
+
+    def bundle(dz):
+        lines = pl.ds(line(2 * dz, 0), 2 * X_RING)
+        return pltpu.make_async_remote_copy(
+            src_ref=send_ref.at[0, lines],
+            dst_ref=mid_ref.at[lines],
+            send_sem=mid_send_sem,
+            recv_sem=mid_recv_sem,
+            device_id={"col": peer(dz, 0)},
+            device_id_type=MESH,
+        )
+
+    def bundles_in():
+        lines = pl.ds(0, (z_ring // 2 - 1) * 2 * X_RING)
+        return pltpu.make_async_remote_copy(
+            src_ref=send_ref.at[0, lines],
+            dst_ref=mid_ref.at[lines],
+            send_sem=mid_send_sem,
+            recv_sem=mid_recv_sem,
+            device_id={"col": peer(1, 0)},
+            device_id_type=MESH,
+        )
+
+    def relay():
+        bundle(z_ring - shift).start()
+
+        def first_leg(i, carry):
+            bundle(shift - i).start()
+            bundle(z_ring - shift + i).start()
+            return carry
+
+        lax.fori_loop(1, shift, first_leg, 0)
+        for dz in (1, z_ring - 1, 0):
+            for dx in OUTER_FIRST:
+                if dz or dx:
+                    start_copy(0, dz, dx, 0)
+        slabs = [slab_copy(0, 0, below), slab_copy(0, 1, above)]
+        for copy in slabs:
+            copy.start()
+        bundles_in().wait_recv()
+        for dx in OUTER_FIRST:
+            start_copy(0, z_ring // 2, dx, 1, z_ring - shift)
+
+        def second_leg(far):
+            def step(i, carry):
+                away = z_ring // 2 - i
+                for dx in OUTER_FIRST:
+                    start_copy(0, away, dx, far, (away + 1) // 2)
+                    start_copy(0, z_ring - away, dx, far, lax.rem(z_ring - away // 2, z_ring))
+                return carry
+
+            return step
+
+        lax.fori_loop(1, z_ring // 2 - shift, second_leg(1), 0)
+        for dx in OUTER_FIRST:
+            start_copy(0, shift, dx, 0, shift // 2)
+            start_copy(0, z_ring - shift, dx, 1, z_ring - shift // 2)
+        lax.fori_loop(z_ring // 2 - shift + 1, z_ring // 2 - 1, second_leg(0), 0)
+        return slabs
 
     def slab_copy(r, side, other):
         part = SLAB // 2
@@ -272,24 +329,28 @@
         given = give(0, n_col)
         send_ref[r, half:n_col, 0:64] = given[0:half]
         send_ref[r, half:n_col, 64:128] = given[half:n_col]
-        for dx in OUTER_FIRST:
-            start_copy(r, z_ring // 2, dx, 1)
-        lax.fori_loop(1, z_ring // 2 - shift, outward(1), 0)
-        for dx in OUTER_FIRST:
-            start_copy(r, shift, dx, 0)
+        if r > 0:
+            for dx in OUTER_FIRST:
+                start_copy(r, z_ring // 2, dx, 1)
+            lax.fori_loop(1, z_ring // 2 - shift, outward(1), 0)
+            for dx in OUTER_FIRST:
+                start_copy(r, shift, dx, 0)
         given = give(n_col, 2 * n_col + 2 * SLAB)
         send_ref[r, 0:half, 0:64] = given[0:half]
         send_ref[r, 0:half, 64:128] = given[half:n_col]
         send_ref[r, n_col:, 0:64] = given[n_col : n_col + SLAB]
         send_ref[r, n_col:, 64:128] = given[n_col + SLAB :]
-        for dx in OUTER_FIRST:
-            start_copy(r, z_ring - shift, dx, 1)
-        lax.fori_loop(z_ring // 2 - shift + 1, z_ring // 2, outward(0), 0)
-        for dx in range(1, X_RING):
-            start_copy(r, 0, dx, 0)
-        slabs = [slab_copy(r, 0, below), slab_copy(r, 1, above)]
-        for copy in slabs:
-            copy.start()
+        if r > 0:
+            for dx in OUTER_FIRST:
+                start_copy(r, z_ring - shift, dx, 1)
+            lax.fori_loop(z_ring // 2 - shift + 1, z_ring // 2, outward(0), 0)
+            for dx in range(1, X_RING):
+                start_copy(r, 0, dx, 0)
+            slabs = [slab_copy(r, 0, below), slab_copy(r, 1, above)]
+            for copy in slabs:
+                copy.start()
+        else:
+            slabs = relay()
 
         cells = field_ref[...]
         cube = cells.reshape(8, 8, 8, LANES)
@@ -357,6 +418,7 @@
     field_ref[...] = second
     finished = 0.5 * (conc_t_ref[...] + section_ref[...] + time_step * laplacian(3))
     next_ref[...] = finished.T[0:blocks]
+    bundles_in().wait_send()
     for r in range(ROUNDS):
         lines_in(r, 0, n_col - 1).wait_send()
         slab_copy(r, 0, below).wait_send()
@@ -394,10 +456,13 @@
                 pltpu.VMEM((FACES, LANES), bf16),
                 pltpu.VMEM((ROUNDS, lines, LANES), f32),
                 pltpu.VMEM((ROUNDS, lines, LANES), f32),
+                pltpu.VMEM((n_col, LANES), f32),
                 pltpu.SemaphoreType.DMA((ROUNDS,)),
                 pltpu.SemaphoreType.DMA((ROUNDS, 2)),
                 pltpu.SemaphoreType.DMA((ROUNDS, 2)),
                 pltpu.SemaphoreType.DMA((ROUNDS, 2)),
+                pltpu.SemaphoreType.DMA,
+                pltpu.SemaphoreType.DMA,
             ],
             compiler_params=pltpu.CompilerParams(
                 collective_id=0, has_side_effects=True, vmem_limit_bytes=32 * 1024 * 1024

time: 88.9 us -> 84.5 us (0.951)
  Pallas kernels: 86.7 us -> 82.3 us
    pallas_call x1, Pallas kernels: 86.7 us -> 82.3 us  [run(): pl.pallas_call(kernel, out_shape=[pltpu.VMEM((blocks, 512), f32)] * 2, in...]
where the time goes in v3:
time: 84.5 us; the launch traced here: 84.4 us
  Pallas kernels  82.3 us (97%)
  local copies, waits for them, and re-layouts  1.39 us (2%)
    pallas_call x1, Pallas kernels, run(): pl.pallas_call(kernel, out_shape=[pltpu.VMEM((blocks, 512), f32)] * 2, in...  82.3 us

profile of v3, /device:TPU:24, one launch (start us, length us, event | category | flops | bytes accessed | tf_op | source)
XLA Modules:
  0.0 84.4 jit_solution(11476900312658850847)
XLA Ops:
  0.6 82.3 %shard_map.68 = (f32[116,512]{1,0:T(8,128)S(1)}, f32[116,512]{1,0:T(8,128)S(1)}) custom-call(f32[116,512]{1,0:T(8,128)} %refs_0_.1, s32[1,116]{1,0:T(1,128)} %bitcast.3, s32[6,116]{1,0:T(8,128)} %refs_2_.1, s32[6,116]{1,0:T(8,128)} %refs_3_.1, s32[8,128]{1,0:T(8,128)} %bitcast.2), custom_call_target="tpu_custom_call" | custom-call | tf_op jit(solution)/shard_map/pallas_call | solution.py:438
  83.0 0.7 copy.9
  83.7 0.7 copy.10

commit v4 on v3

--- a/solution.py
+++ b/solution.py
@@ -54,10 +54,10 @@
 def body(
     n_row, n_col,
     conc_ref, levels_ref, nb_ref, hang_ref, counts_ref,
-    next_ref, pot_ref,
+    out_ref,
     conc_in, pad_ref, levels_in, nb_in, hang_in, counts_in, load_sem,
     ints_ref, off_ref, field_ref, conc_t_ref, section_ref, inner_ref, zbuf_ref, give_ref, take_ref, local_ref,
-    send_ref, recv_ref, mid_ref, send_sem, recv_sem, slab_send_sem, slab_recv_sem, mid_send_sem, mid_recv_sem,
+    send_ref, recv_ref, mid_ref, send_sem, recv_sem, slab_send_sem, slab_recv_sem, mid_send_sem, mid_recv_sem, hello_sem,
 ):
     blocks = conc_ref.shape[0]
     z_ring = n_col // X_RING
@@ -86,10 +86,8 @@
         pl.semaphore_signal(barrier, inc=1, device_id={"col": peer(dz, dx)}, device_id_type=MESH)
 
     def greet_pair(i, carry):
-        away = shift + 1 - i
-        for dx in OUTER_FIRST:
-            greet(away, dx)
-            greet(z_ring - away, dx)
+        greet(shift + 1 - i, 0)
+        greet(z_ring - shift - 1 + i, 0)
         return carry
 
     lax.fori_loop(1, shift + 1, greet_pair, 0)
@@ -208,7 +206,6 @@
         ref[2 * n_col + SLAB : 2 * n_col + 2 * SLAB, :] = onehot(slab_id + SLAB // 2 == place)
     zbuf_ref[...] = jnp.zeros((512, LANES), f32)
 
-    pl.semaphore_wait(barrier, (2 * shift + 1) * X_RING + 1)
 
     def start_copy(r, dz, dx, far, left=None):
         pltpu.make_async_remote_copy(
@@ -243,7 +240,9 @@
         )
 
     def relay():
+        pl.semaphore_wait(barrier, 2 * shift + X_RING - 1 + 2)
         bundle(z_ring - shift).start()
+        pl.semaphore_signal(hello_sem, inc=1, device_id={"col": peer(shift, 0)}, device_id_type=MESH)
 
         def first_leg(i, carry):
             bundle(shift - i).start()
@@ -251,13 +250,10 @@
             return carry
 
         lax.fori_loop(1, shift, first_leg, 0)
-        for dz in (1, z_ring - 1, 0):
-            for dx in OUTER_FIRST:
-                if dz or dx:
-                    start_copy(0, dz, dx, 0)
         slabs = [slab_copy(0, 0, below), slab_copy(0, 1, above)]
         for copy in slabs:
             copy.start()
+        pl.semaphore_wait(hello_sem, 1)
         bundles_in().wait_recv()
         for dx in OUTER_FIRST:
             start_copy(0, z_ring // 2, dx, 1, z_ring - shift)
@@ -277,6 +273,10 @@
             start_copy(0, shift, dx, 0, shift // 2)
             start_copy(0, z_ring - shift, dx, 1, z_ring - shift // 2)
         lax.fori_loop(z_ring // 2 - shift + 1, z_ring // 2 - 1, second_leg(0), 0)
+        for dz in (1, z_ring - 1, 0):
+            for dx in OUTER_FIRST:
+                if dz or dx:
+                    start_copy(0, dz, dx, 0)
         return slabs
 
     def slab_copy(r, side, other):
@@ -376,7 +376,12 @@
         ghosts = jnp.concatenate(near_ghosts, axis=1)
 
         if r == ROUNDS - 1:
-            pot_ref[...] = cells.T[0:blocks]
+            out_ref[1] = cells.T
+            bundles_in().wait_send()
+            for done in range(ROUNDS):
+                lines_in(done, 0, n_col - 1).wait_send()
+                slab_copy(done, 0, below).wait_send()
+                slab_copy(done, 1, above).wait_send()
 
         lines_in(r, 0, half - 1).wait_recv()
         for copy in slabs:
@@ -417,12 +422,7 @@
     second = potential(section_ref[...], laplacian(2))
     field_ref[...] = second
     finished = 0.5 * (conc_t_ref[...] + section_ref[...] + time_step * laplacian(3))
-    next_ref[...] = finished.T[0:blocks]
-    bundles_in().wait_send()
-    for r in range(ROUNDS):
-        lines_in(r, 0, n_col - 1).wait_send()
-        slab_copy(r, 0, below).wait_send()
-        slab_copy(r, 1, above).wait_send()
+    out_ref[0] = finished.T
 
 
 def per_device(n_row, n_col):
@@ -435,11 +435,11 @@
         def kernel(*refs):
             body(n_row, n_col, *refs)
 
-        return pl.pallas_call(
+        both = pl.pallas_call(
             kernel,
-            out_shape=[pltpu.VMEM((blocks, 512), f32)] * 2,
+            out_shape=pltpu.VMEM((2, LANES, 512), f32),
             in_specs=[pl.BlockSpec(memory_space=pltpu.HBM)] * 5,
-            out_specs=[vmem] * 2,
+            out_specs=vmem,
             scratch_shapes=[
                 pltpu.VMEM((blocks, 512), f32),
                 pltpu.VMEM((LANES, 512), f32),
@@ -463,6 +463,7 @@
                 pltpu.SemaphoreType.DMA((ROUNDS, 2)),
                 pltpu.SemaphoreType.DMA,
                 pltpu.SemaphoreType.DMA,
+                pltpu.SemaphoreType.REGULAR,
             ],
             compiler_params=pltpu.CompilerParams(
                 collective_id=0, has_side_effects=True, vmem_limit_bytes=32 * 1024 * 1024
@@ -473,6 +474,7 @@
                 for v in (conc, levels.reshape(1, blocks), neighbours, hanging, block_counts.reshape(n_row, n_col))
             )
         )
+        return both[0, :blocks], both[1, :blocks]
 
     return run
 

time: 84.5 us -> 81.6 us (0.966)
  Pallas kernels: 82.3 us -> 80 us
    pallas_call x1, Pallas kernels: 82.3 us -> 80 us  [run(): pl.pallas_call(kernel, out_shape=pltpu.VMEM((2, LANES, 512), f32), in_spe...]
    unnamed x2 -> x0, local copies, waits for them, and re-layouts: 1.39 us -> none
where the time goes in v4:
time: 81.6 us; the launch traced here: 81.5 us
  Pallas kernels  80 us (98%)
    pallas_call x1, Pallas kernels, run(): pl.pallas_call(kernel, out_shape=pltpu.VMEM((2, LANES, 512), f32), in_spe...  80 us

profile of v4, /device:TPU:24, one launch (start us, length us, event | category | flops | bytes accessed | tf_op | source)
XLA Modules:
  0.0 81.5 jit_solution(16831579726526179061)
XLA Ops:
  0.6 80.0 %shard_map.68 = f32[2,128,512]{2,1,0:T(8,128)S(1)} custom-call(f32[116,512]{1,0:T(8,128)} %refs_0_.1, s32[1,116]{1,0:T(1,128)} %bitcast.7, s32[6,116]{1,0:T(8,128)} %refs_2_.1, s32[6,116]{1,0:T(8,128)} %refs_3_.1, s32[8,128]{1,0:T(8,128)} %bitcast.6), custom_call_target="tpu_custom_call" | custom-call | tf_op jit(solution)/shard_map/pallas_call | solution.py:438
  80.7 0.8 slice_bitcast_fusion

commit v5 on v4

--- a/solution.py
+++ b/solution.py
@@ -55,7 +55,7 @@
     n_row, n_col,
     conc_ref, levels_ref, nb_ref, hang_ref, counts_ref,
     out_ref,
-    conc_in, pad_ref, levels_in, nb_in, hang_in, counts_in, load_sem,
+    give_t_ref, conc_in, pad_ref, levels_in, nb_in, hang_in, counts_in, load_sem,
     ints_ref, off_ref, field_ref, conc_t_ref, section_ref, inner_ref, zbuf_ref, give_ref, take_ref, local_ref,
     send_ref, recv_ref, mid_ref, send_sem, recv_sem, slab_send_sem, slab_recv_sem, mid_send_sem, mid_recv_sem, hello_sem,
 ):
@@ -205,6 +205,7 @@
         ref[2 * n_col : 2 * n_col + SLAB, :] = onehot(slab_id == place)
         ref[2 * n_col + SLAB : 2 * n_col + 2 * SLAB, :] = onehot(slab_id + SLAB // 2 == place)
     zbuf_ref[...] = jnp.zeros((512, LANES), f32)
+    give_t_ref[...] = give_ref[0:n_col, :].astype(f32).T.astype(bf16)
 
 
     def start_copy(r, dz, dx, far, left=None):
@@ -304,18 +305,20 @@
         return v[0:64] + (v[64:128] + v[128:192])
 
     def by_cell(lines):
-        turned_lines = lines.T
-        return jnp.concatenate([turned_lines[0:64], turned_lines[64:128]], axis=1)
+        return jnp.concatenate([lines[:, 0:64], lines[:, 64:128]], axis=0).T
 
     def laplacian(r):
         layers = layer_parts(field_ref)
         cut = pieces(jnp.concatenate(layers, axis=1))
 
         def give(first, last):
-            given = lax.dot_general(
-                give_ref[first:last, :], cut, (((1,), (1,)), ((), ())), preferred_element_type=f32
-            )
-            return given[:, 0:64] + (given[:, 64:128] + given[:, 128:192])
+            if first:
+                given = lax.dot_general(
+                    give_ref[first:last, :], cut, (((1,), (1,)), ((), ())), preferred_element_type=f32
+                )
+                return given[:, 0:64] + (given[:, 64:128] + given[:, 128:192])
+            given = summed(jnp.dot(cut, give_t_ref[...], preferred_element_type=f32))
+            return jnp.concatenate([given[:, 0:half], given[:, half:n_col]], axis=0).T
 
         def outward(far):
             def step(away, carry):
@@ -327,8 +330,7 @@
             return lambda i, carry: step(z_ring // 2 - i, carry)
 
         given = give(0, n_col)
-        send_ref[r, half:n_col, 0:64] = given[0:half]
-        send_ref[r, half:n_col, 64:128] = given[half:n_col]
+        send_ref[r, half:n_col, :] = given
         if r > 0:
             for dx in OUTER_FIRST:
                 start_copy(r, z_ring // 2, dx, 1)
@@ -441,6 +443,7 @@
             in_specs=[pl.BlockSpec(memory_space=pltpu.HBM)] * 5,
             out_specs=vmem,
             scratch_shapes=[
+                pltpu.VMEM((FACES, n_col), bf16),
                 pltpu.VMEM((blocks, 512), f32),
                 pltpu.VMEM((LANES, 512), f32),
                 pltpu.VMEM((1, blocks), jnp.int32),

time: 81.6 us -> 81 us (level)
  no operation moved by 1% of the time
where the time goes in v5:
time: 81 us; the launch traced here: 80.9 us
  Pallas kernels  79.4 us (98%)
  local copies, waits for them, and re-layouts  0.81 us (1%)
    pallas_call x1, Pallas kernels, run(): pl.pallas_call(kernel, out_shape=pltpu.VMEM((2, LANES, 512), f32), in_spe...  79.4 us

profile of v5, /device:TPU:24, one launch (start us, length us, event | category | flops | bytes accessed | tf_op | source)
XLA Modules:
  0.0 80.9 jit_solution(11072326918310138472)
XLA Ops:
  0.6 79.4 %shard_map.68 = f32[2,128,512]{2,1,0:T(8,128)S(1)} custom-call(f32[116,512]{1,0:T(8,128)} %refs_0_.1, s32[1,116]{1,0:T(1,128)} %bitcast.7, s32[6,116]{1,0:T(8,128)} %refs_2_.1, s32[6,116]{1,0:T(8,128)} %refs_3_.1, s32[8,128]{1,0:T(8,128)} %bitcast.6), custom_call_target="tpu_custom_call" | custom-call | tf_op jit(solution)/shard_map/pallas_call | solution.py:440
  80.1 0.8 slice_bitcast_fusion
